TPU v7x, 32 devices: a whole 2x2x4 slice. The times are simulated.
32 devices in a mesh: dp: 16 (over z, y, core), tensor: 2 (over x).
Axes of the slice: x: 2, y: 2, z: 4, core: 2. Of those that a mesh axis runs over, the one named last changes fastest.
Arguments:
- inputs: bfloat16 [32768, 768], P(('dp', 'tensor')), may hold values from -6 to 6
- gain_attn: bfloat16 [768], replicated, may hold values from 0.5 to 1.5
- w_query: bfloat16 [768, 768], P(None, 'tensor'), may hold values from -0.09375 to 0.09375
- w_key: bfloat16 [768, 768], P(None, 'tensor'), may hold values from -0.09375 to 0.09375
- w_value: bfloat16 [768, 768], P(None, 'tensor'), may hold values from -0.21875 to 0.21875
- w_output: bfloat16 [768, 768], P('tensor'), may hold values from -0.875 to 0.875
- relative_bias_table: bfloat16 [32, 12], P(None, 'tensor'), may hold values from -4 to 4
- gain_ffn: bfloat16 [768], replicated, may hold values from 0.5 to 1.5
- w_inner: bfloat16 [768, 3072], P(None, 'tensor'), may hold values from -0.21875 to 0.21875
- w_outer: bfloat16 [3072, 768], P('tensor'), may hold values from -0.109375 to 0.109375
- lengths: int32 [128], P('dp'), may hold values from 40 to 256, as said below
- cotangent: bfloat16 [32768, 768], P(('dp', 'tensor')), may hold values from -6 to 6
Outputs:
- layer_out: bfloat16 [32768, 768], P(('dp', 'tensor'))
- grad_input: float32 [32768, 768], P(('dp', 'tensor'))
- grad_gain_attn: float32 [768], replicated
- grad_query: float32 [768, 768], P('dp', 'tensor')
- grad_key: float32 [768, 768], P('dp', 'tensor')
- grad_value: float32 [768, 768], P('dp', 'tensor')
- grad_output: float32 [768, 768], P('tensor', 'dp')
- grad_table: float32 [32, 12], P(None, 'tensor')
- grad_gain_ffn: float32 [768], replicated
- grad_inner: float32 [768, 3072], P('dp', 'tensor')
- grad_outer: float32 [3072, 768], P('tensor', 'dp')
Inputs may be any that keep to these rules, and one draw needn't show every extreme that they name: Each passage's valid keys are its first lengths slots; in every draw some passage has all 256 slots valid and some has the fewest.
All inputs are finite; a program needn't handle non-finite values.
Results may differ from a plain program's by a relative error of at most 0.013.
The roundings to bfloat16 on the way count: a program that leaves them out, or rounds other values in their place, can miss the bound.
Values may be sent and summed in bfloat16 or wider, within the bound.
No kernel may reach another device: no remote copies, remote signals or barrier semaphores. Data moves between devices by JAX's collectives and lax.ppermute only.
A program may use at most 192 MiB of HBM per device.

v0:
```python
import jax
import jax.numpy as jnp
from jax import lax
from jax.sharding import PartitionSpec as P

HEAD_DIM = 64
BUCKETS = 32


def rms_norm(values, gain):
    return values * lax.rsqrt(jnp.mean(values * values, axis=-1, keepdims=True) + 1e-06) * gain


def bucket_ids(seq_len):
    positions = jnp.arange(seq_len, dtype=jnp.int32)
    offsets = positions[None, :] - positions[:, None]
    distance = jnp.abs(offsets)
    far_bucket = jnp.full_like(distance, 8)
    for power in range(1, 8):
        far_bucket = far_bucket + (distance * distance >= 64 * 2**power).astype(jnp.int32)
    near_bucket = jnp.where(distance < 8, distance, far_bucket)
    return near_bucket + 16 * (offsets > 0).astype(jnp.int32)


def gather_rows(values):
    return lax.all_gather(values, "tensor", axis=0, tiled=True)


def sum_branch(values):
    return lax.psum_scatter(values, "tensor", scatter_dimension=0, tiled=True)


def gather_grads(values):
    return lax.all_gather(values, "tensor", axis=0, tiled=True)


def sum_back(values):
    return lax.psum_scatter(values, "tensor", scatter_dimension=0, tiled=True)


def matmul(left, right):
    return jnp.dot(left, right, preferred_element_type=jnp.float32)


def shards(
    inputs,
    gain_attn,
    w_query,
    w_key,
    w_value,
    w_output,
    relative_bias_table,
    gain_ffn,
    w_inner,
    w_outer,
    lengths,
    cotangent,
):
    passages = lengths.shape[0]
    width_local = w_query.shape[1]
    head_count = width_local // HEAD_DIM
    inputs_f = inputs.astype(jnp.float32)
    gain_one = gain_attn.astype(jnp.float32)
    gain_two = gain_ffn.astype(jnp.float32)
    normed_one, norm_back_one = jax.vjp(rms_norm, inputs_f, gain_one)
    rows_one = gather_rows(normed_one.astype(jnp.bfloat16))
    all_rows = rows_one.shape[0]
    seq_len = all_rows // passages
    per_block = min(passages, max(1, 512 // seq_len))
    block_count = passages // per_block
    shape_five = (block_count, per_block, seq_len, head_count, HEAD_DIM)
    query = matmul(rows_one, w_query).astype(jnp.bfloat16)
    keyset = matmul(rows_one, w_key).astype(jnp.bfloat16)
    values = matmul(rows_one, w_value).astype(jnp.bfloat16)
    query_five = query.reshape(shape_five)
    key_five = keyset.reshape(shape_five)
    value_five = values.reshape(shape_five)
    bucket_indicator = (
        bucket_ids(seq_len)[None, :, :] == jnp.arange(BUCKETS, dtype=jnp.int32)[:, None, None]
    ).astype(jnp.bfloat16)
    expanded_bias = jnp.einsum(
        "utc,ul->ltc", bucket_indicator, relative_bias_table, preferred_element_type=jnp.float32
    )
    key_mask = (jnp.arange(seq_len, dtype=jnp.int32)[None, :] < lengths[:, None]).reshape(
        block_count, per_block, seq_len
    )

    def score_fn(part_q, part_k, part_m):
        logits = (
            jnp.einsum("gqhe,gkhe->ghqk", part_q, part_k, preferred_element_type=jnp.float32)
            + expanded_bias
        )
        return jnp.where(part_m[:, None, None, :], logits, -1000000000.0)

    def attend(pieces):
        part_q, part_k, part_v, part_m = pieces
        logits = score_fn(part_q, part_k, part_m)
        peak = jnp.max(logits, axis=-1, keepdims=True)
        exp_terms = jnp.exp(logits - peak)
        denom_sum = jnp.sum(exp_terms, axis=-1, keepdims=True)
        probs = exp_terms / denom_sum
        context_block = jnp.einsum(
            "ghqk,gkhe->gqhe",
            probs.astype(jnp.bfloat16),
            part_v,
            preferred_element_type=jnp.float32,
        )
        return (context_block.astype(jnp.bfloat16), (peak + jnp.log(denom_sum))[..., 0])

    context, log_total = lax.map(attend, (query_five, key_five, value_five, key_mask))
    context = context.reshape(all_rows, width_local)
    attn_out = sum_branch(matmul(context, w_output))
    residual = inputs_f + attn_out
    normed_two, norm_back_two = jax.vjp(rms_norm, residual, gain_two)
    rows_two = gather_rows(normed_two.astype(jnp.bfloat16))
    pre_act = matmul(rows_two, w_inner)
    act_val, act_back = jax.vjp(jax.nn.gelu, pre_act)
    active = act_val.astype(jnp.bfloat16)
    ffn_out = sum_branch(matmul(active, w_outer))
    layer_out = (residual + ffn_out).astype(jnp.bfloat16)
    grad_top = cotangent.astype(jnp.float32)
    grad_ffn = gather_grads(grad_top.astype(jnp.bfloat16))
    grad_outer = jnp.einsum("rf,rd->fd", active, grad_ffn, preferred_element_type=jnp.float32)
    grad_active = jnp.einsum("rd,fd->rf", grad_ffn, w_outer, preferred_element_type=jnp.float32)
    grad_pre = act_back(grad_active)[0].astype(jnp.bfloat16)
    grad_inner = jnp.einsum("rd,rf->df", rows_two, grad_pre, preferred_element_type=jnp.float32)
    back_part_two = jnp.einsum("rf,df->rd", grad_pre, w_inner, preferred_element_type=jnp.float32)
    grad_normed_two = sum_back(back_part_two)
    back_resid, grad_gain_two = norm_back_two(grad_normed_two)
    grad_residual = grad_top + back_resid
    grad_attn = gather_grads(grad_residual.astype(jnp.bfloat16))
    grad_output = jnp.einsum("rc,rd->cd", context, grad_attn, preferred_element_type=jnp.float32)
    grad_context = jnp.einsum(
        "rd,cd->rc", grad_attn, w_output, preferred_element_type=jnp.float32
    ).astype(jnp.bfloat16)

    def attend_back(pieces):
        part_q, part_k, part_v, part_m, part_l, part_g = pieces
        logits = score_fn(part_q, part_k, part_m)
        probs = jnp.exp(logits - part_l[..., None])
        grad_probs = jnp.einsum(
            "gqhe,gkhe->ghqk", part_g, part_v, preferred_element_type=jnp.float32
        )
        logits_gradient = probs * (grad_probs - jnp.sum(probs * grad_probs, axis=-1, keepdims=True))
        grad_low = logits_gradient.astype(jnp.bfloat16)
        grad_q = jnp.einsum("ghqk,gkhe->gqhe", grad_low, part_k, preferred_element_type=jnp.float32)
        grad_k = jnp.einsum("ghqk,gqhe->gkhe", grad_low, part_q, preferred_element_type=jnp.float32)
        grad_v = jnp.einsum(
            "ghqk,gqhe->gkhe",
            probs.astype(jnp.bfloat16),
            part_g,
            preferred_element_type=jnp.float32,
        )
        bias_part = jnp.sum(grad_low.astype(jnp.float32), axis=0)
        return (
            grad_q.astype(jnp.bfloat16),
            grad_k.astype(jnp.bfloat16),
            grad_v.astype(jnp.bfloat16),
            bias_part,
        )

    grad_q5, grad_k5, grad_v5, bias_parts = lax.map(
        attend_back,
        (query_five, key_five, value_five, key_mask, log_total, grad_context.reshape(shape_five)),
    )
    grad_q_rows = grad_q5.reshape(all_rows, width_local)
    grad_k_rows = grad_k5.reshape(all_rows, width_local)
    grad_v_rows = grad_v5.reshape(all_rows, width_local)
    grad_table = jnp.einsum(
        "acw,lcw->al",
        bucket_indicator.astype(jnp.float32),
        jnp.sum(bias_parts, axis=0),
        precision=lax.Precision.HIGHEST,
    )
    grad_query = jnp.einsum("rd,rc->dc", rows_one, grad_q_rows, preferred_element_type=jnp.float32)
    grad_key = jnp.einsum("rd,rc->dc", rows_one, grad_k_rows, preferred_element_type=jnp.float32)
    grad_value = jnp.einsum("rd,rc->dc", rows_one, grad_v_rows, preferred_element_type=jnp.float32)
    grad_rows_sum = jnp.einsum(
        "rc,dc->rd", grad_q_rows, w_query, preferred_element_type=jnp.float32
    )
    grad_rows_sum = grad_rows_sum + jnp.einsum(
        "rc,dc->rd", grad_k_rows, w_key, preferred_element_type=jnp.float32
    )
    grad_rows_sum = grad_rows_sum + jnp.einsum(
        "rc,dc->rd", grad_v_rows, w_value, preferred_element_type=jnp.float32
    )
    grad_normed_one = sum_back(grad_rows_sum)
    back_input, grad_gain_one = norm_back_one(grad_normed_one)
    grad_input = grad_residual + back_input
    grad_table = lax.psum(grad_table, "dp")
    grad_gain_one, grad_gain_two = lax.psum((grad_gain_one, grad_gain_two), ("dp", "tensor"))
    grad_query, grad_key, grad_value, grad_output, grad_inner, grad_outer = (
        lax.psum_scatter(grad_query, "dp", scatter_dimension=0, tiled=True),
        lax.psum_scatter(grad_key, "dp", scatter_dimension=0, tiled=True),
        lax.psum_scatter(grad_value, "dp", scatter_dimension=0, tiled=True),
        lax.psum_scatter(grad_output, "dp", scatter_dimension=1, tiled=True),
        lax.psum_scatter(grad_inner, "dp", scatter_dimension=0, tiled=True),
        lax.psum_scatter(grad_outer, "dp", scatter_dimension=1, tiled=True),
    )
    return (
        layer_out,
        grad_input,
        grad_gain_one,
        grad_query,
        grad_key,
        grad_value,
        grad_output,
        grad_table,
        grad_gain_two,
        grad_inner,
        grad_outer,
    )


def solution(mesh):
    in_specs = (
        P(("dp", "tensor"), None),
        P(),
        P(None, "tensor"),
        P(None, "tensor"),
        P(None, "tensor"),
        P("tensor", None),
        P(None, "tensor"),
        P(),
        P(None, "tensor"),
        P("tensor", None),
        P("dp"),
        P(("dp", "tensor"), None),
    )
    out_specs = (
        P(("dp", "tensor"), None),
        P(("dp", "tensor"), None),
        P(),
        P("dp", "tensor"),
        P("dp", "tensor"),
        P("dp", "tensor"),
        P("tensor", "dp"),
        P(None, "tensor"),
        P(),
        P("dp", "tensor"),
        P("tensor", "dp"),
    )
    return jax.shard_map(shards, mesh=mesh, in_specs=in_specs, out_specs=out_specs, check_vma=False)
```

profile of v0, /device:TPU:0, one launch (start us, length us, event | category | flops | bytes accessed | tf_op | source)
XLA Modules:
  0.0 1153.9 jit_solution(7090414725302451278)
XLA Ops:
  20.8 41.1 %all-gather.5.cloned.1.call-done = bf16[2048,768]{1,0:T(8,128)(2,1)} async-done(((bf16[1024,768]{1,0:T(8,128)(2,1)}), bf16[2048,768]{1,0:T(8,128)(2,1)}) %all-gather.5.cloned.1.call-update) | async-done | bytes 3145744 | tf_op jit(solution)/shard_map/all_gather | solution.py:26
  61.9 4.8 convolution_convert_fusion.3
  69.3 3.9 reshape.170
  73.2 3.1 copy.66
  81.8 3.9 reshape.169
  94.3 3.8 reshape.168
  103.0 25.7 %while.28 = (s32[]{:T(128)}, bf16[4,2,256,6,64]{2,1,0,4,3:T(2,128)(2,1)}, f32[4,2,6,256]{3,2,1,0:T(8,128)S(1)}, bf16[4,2,256,6,64]{2,4,3,1,0:T(8,128)(2,1)}, pre...) while((s32[]{:T(128)}, ...), condition=%wide.region_4.5_spmd, body=%wide.region_1.4_spmd.sunk | while | flops 210957312 | bytes 22920848 | solution.py:110
  128.7 4.3 reshape.171
  133.0 5.9 fusion.78
  139.6 76.6 %reduce-scatter.11.cloned.1.call-done = f32[1024,768]{1,0:T(8,128)} async-done(((f32[2048,768]{1,0:T(8,128)}), f32[1024,768]{1,0:T(8,128)}) %reduce-scatter.11.cloned.1.call-update) | async-done | bytes 3145744 | tf_op jit(solution)/shard_map/reduce_scatter | solution.py:30
  222.8 44.5 %all-gather.7.cloned.1.call-done = bf16[2048,768]{1,0:T(8,128)(2,1)} async-done(((bf16[1024,768]{1,0:T(8,128)(2,1)}), bf16[2048,768]{1,0:T(8,128)(2,1)}) %all-gather.7.cloned.1.call-update) | async-done | bytes 3145744 | tf_op jit(solution)/shard_map/all_gather | solution.py:26
  267.2 13.0 %multiply_convert_fusion.1 = (bf16[2048,1536]{1,0:T(8,128)(2,1)}, f32[2048,1536]{1,0:T(8,128)}) fusion(bf16[2048,768]{1,0:T(8,128)(2,1)} %all-gather.7.cloned.1.call-done, bf16[768,1536]{1,0:T(8,128)(2,1)S(1)} %copy-done), kind=kOutput, calls=%fused_computation.65 | convolution fusion | flops 4860149760 | bytes 24379392 | tf_op jit(solution)/shard_map/dot_general | solution.py:42
  280.2 33.5 %all-gather.9.cloned.1.call-done = bf16[2048,768]{1,0:T(8,128)(2,1)} async-done(((bf16[1024,768]{1,0:T(8,128)(2,1)}), bf16[2048,768]{1,0:T(8,128)(2,1)}) %all-gather.9.cloned.1.call-update) | async-done | bytes 3145744 | tf_op jit(solution)/shard_map/all_gather | solution.py:34
  313.7 15.6 %fusion.46 = bf16[2048,1536]{1,0:T(8,128)(2,1)S(1)} fusion(f32[2048,1536]{1,0:T(8,128)} %get-tuple-element.244, bf16[2048,768]{1,0:T(8,128)(2,1)} %all-gather.9.cloned.1.call-done, bf16[1536,768]{1,0:T(8,128)(2,1)} %param.25), kind=kOutput, calls=%fused_computation.64 | convolution fusion | flops 4894752768 | bytes 24379392 | tf_op jit(solution)/shard_map/rd,fd->rf/dot_general | solution.py:124
  332.0 6.9 fusion.80
  339.0 77.1 %reduce-scatter.15.cloned.1.call-done = f32[1024,768]{1,0:T(8,128)} async-done(((f32[2048,768]{1,0:T(8,128)}), f32[1024,768]{1,0:T(8,128)}) %reduce-scatter.15.cloned.1.call-update) | async-done | bytes 3145744 | tf_op jit(solution)/shard_map/reduce_scatter | solution.py:38
  416.2 3.8 multiply_reduce_fusion.1
  420.0 3.9 fusion.77
  424.1 44.9 %all-gather.11.cloned.1.call-done = bf16[2048,768]{1,0:T(8,128)(2,1)} async-done(((bf16[1024,768]{1,0:T(8,128)(2,1)}), bf16[2048,768]{1,0:T(8,128)(2,1)}) %all-gather.11.cloned.1.call-update) | async-done | bytes 3145744 | tf_op jit(solution)/shard_map/all_gather | solution.py:34
  469.0 4.9 convolution_convert_fusion.2
  483.8 81.6 %while.29 = (s32[]{:T(128)}, bf16[4,2,256,6,64]{2,1,0,4,3:T(2,128)(2,1)}, bf16[4,2,256,6,64]{2,1,0,4,3:T(2,128)(2,1)}, bf16[4,2,256,6,64]{2,1,0,4,3:T(2,128)(2,1...) while((s32[]{:T(128)}, ...), condition=%wide.region_13.14_spmd, body=%wide.region_10.13_spmd.sunk | while | flops 512160768 | bytes 46463684 | solution.py:162
  489.0 3.1 convert_reduce_fusion.2
  492.7 3.1 copy.124
  513.2 3.1 copy.124
  533.5 3.1 copy.124
  554.0 3.1 copy.124
  565.4 3.8 reshape.173
  572.2 4.0 reshape.175
  580.0 4.7 add_add_fusion
  584.7 9.5 fusion.79
  594.3 10.0 fusion.88
  604.4 10.1 fusion.87
  614.5 5.3 fusion.86
  619.8 5.3 fusion.83
  625.2 4.8 fusion.84
  630.2 5.2 fusion.85
  635.5 4.7 reduce_sum.100
  640.2 5.9 fusion.61
  646.1 33.7 %psum.22 = f32[32,6]{0,1:T(8,128)} all-reduce(f32[32,6]{0,1:T(8,128)S(1)} %fusion.61), channel_id=1, replica_groups=mesh['dp'=16,'tensor'=2] {'dp'}, use_global_device_ids=true, to_apply=%region_23.24 | all-reduce | flops 192 | bytes 1536 | tf_op jit(solution)/shard_map/psum | solution.py:190
  682.8 37.5 %all-reduce = (f32[768]{0:T(1024)}, f32[768]{0:T(1024)}) all-reduce(f32[768]{0:T(1024)S(1)} %get-tuple-element.187, f32[768]{0:T(1024)S(1)} %get-tuple-element.185), channel_id=1, replica_groups=mesh['dp'=16,'tensor'=2] {'dp','tensor'}, use_global_device_ids=true, to_apply=%region_17.18 | all-reduce | flops 1536 | bytes 12288 | tf_op jit(solution)/shard_map/psum | solution.py:191
  720.3 22.5 %reduce-scatter.13.cloned.1.call-done = f32[1024,768]{1,0:T(8,128)} async-done(((f32[2048,768]{1,0:T(8,128)}), f32[1024,768]{1,0:T(8,128)}) %reduce-scatter.13.cloned.1.call-update) | async-done | bytes 3145744 | tf_op jit(solution)/shard_map/reduce_scatter | solution.py:30
  742.8 8.8 fusion.56
  751.6 71.2 %reduce-scatter.29.cloned.1.call-done = f32[1536,48]{0,1:T(8,128)} async-done(((f32[1536,768]{0,1:T(8,128)}), f32[1536,48]{0,1:T(8,128)}) %reduce-scatter.29.cloned.1.call-update) | async-done | bytes 294928 | tf_op jit(solution)/shard_map/reduce_scatter | solution.py:198
  822.8 79.4 %reduce-scatter.27.cloned.1.call-done = f32[48,1536]{1,0:T(8,128)} async-done(((f32[768,1536]{1,0:T(8,128)}), f32[48,1536]{1,0:T(8,128)}) %reduce-scatter.27.cloned.1.call-update) | async-done | bytes 294928 | tf_op jit(solution)/shard_map/reduce_scatter | solution.py:197
  902.3 61.3 %reduce-scatter.25.cloned.1.call-done = f32[384,48]{0,1:T(8,128)} async-done(((f32[384,768]{0,1:T(8,128)}), f32[384,48]{0,1:T(8,128)}) %reduce-scatter.25.cloned.1.call-update) | async-done | bytes 73744 | tf_op jit(solution)/shard_map/reduce_scatter | solution.py:196
  963.6 61.1 %reduce-scatter.19.cloned.1.call-done = f32[48,384]{1,0:T(8,128)} async-done(((f32[768,384]{1,0:T(8,128)}), f32[48,384]{1,0:T(8,128)}) %reduce-scatter.19.cloned.1.call-update) | async-done | bytes 73744 | tf_op jit(solution)/shard_map/reduce_scatter | solution.py:193
  1024.7 61.3 %reduce-scatter.21.cloned.1.call-done = f32[48,384]{1,0:T(8,128)} async-done(((f32[768,384]{1,0:T(8,128)}), f32[48,384]{1,0:T(8,128)}) %reduce-scatter.21.cloned.1.call-update) | async-done | bytes 73744 | tf_op jit(solution)/shard_map/reduce_scatter | solution.py:194
  1086.0 61.1 %reduce-scatter.23.cloned.1.call-done = f32[48,384]{1,0:T(8,128)} async-done(((f32[768,384]{1,0:T(8,128)}), f32[48,384]{1,0:T(8,128)}) %reduce-scatter.23.cloned.1.call-update) | async-done | bytes 73744 | tf_op jit(solution)/shard_map/reduce_scatter | solution.py:195
  (210 shorter events, 157.1 us)
Async XLA Ops:
  7.2 260.1 %copy-start = (bf16[768,1536]{1,0:T(8,128)(2,1)S(1)}, bf16[768,1536]{1,0:T(8,128)(2,1)}, u32[]{:S(2)}) copy-start(bf16[768,1536]{1,0:T(8,128)(2,1)} %param.24) | copy-start | bytes 7077892
  7.2 54.7 %all-gather.5.cloned.1.call-start = ((), (), s32[]{:S(2)}) async-start(), calls=%async_computation.10 | async-start | bytes 4718592 | tf_op jit(solution)/shard_map/all_gather | solution.py:26
  8.1 2.4 copy-start.20
  8.1 6.1 copy-start.28
  8.1 7.1 copy-start.27
  14.1 202.1 %reduce-scatter.11.cloned.1.call-start = ((), (), s32[]{:S(2)}) async-start(), calls=%async_computation.11 | async-start | bytes 9437184 | tf_op jit(solution)/shard_map/reduce_scatter | solution.py:30
  14.2 47.6 %copy-start.14 = (bf16[768,384]{1,0:T(8,128)(2,1)S(1)}, bf16[768,384]{1,0:T(8,128)(2,1)}, u32[]{:S(2)}) copy-start(bf16[768,384]{1,0:T(8,128)(2,1)} %param.19) | copy-start | bytes 1769476
  69.3 7.0 copy-start.16
  73.2 3.1 copy-start.29
  81.8 7.0 copy-start.18
  85.7 3.1 copy-start.30
  103.0 2.5 copy-start.2
  109.4 2.5 copy-start.2
  115.9 2.5 copy-start.2
  122.3 2.5 copy-start.2
  128.7 4.3 copy-start.13
  138.9 128.3 %all-gather.7.cloned.1.call-start = ((), (), s32[]{:S(2)}) async-start(), calls=%async_computation.12 | async-start | bytes 4718592 | tf_op jit(solution)/shard_map/all_gather | solution.py:26
  219.0 1.7 copy-start.5
  222.2 91.5 %all-gather.9.cloned.1.call-start = ((), (), s32[]{:S(2)}) async-start(), calls=%async_computation.14 | async-start | bytes 4718592 | tf_op jit(solution)/shard_map/all_gather | solution.py:34
  222.7 193.4 %reduce-scatter.15.cloned.1.call-start = ((), (), s32[]{:S(2)}) async-start(), calls=%async_computation.15 | async-start | bytes 9437184 | tf_op jit(solution)/shard_map/reduce_scatter | solution.py:38
  329.3 2.7 copy-start.31
  339.0 81.0 %copy-start.8 = (bf16[1024,768]{1,0:T(8,128)(2,1)S(1)}, bf16[1024,768]{1,0:T(8,128)(2,1)}, u32[]{:S(2)}) copy-start(bf16[1024,768]{1,0:T(8,128)(2,1)} %param.27) | copy-start | bytes 4718596
  339.0 130.0 %all-gather.11.cloned.1.call-start = ((), (), s32[]{:S(2)}) async-start(), calls=%async_computation.16 | async-start | bytes 4718592 | tf_op jit(solution)/shard_map/all_gather | solution.py:34
  416.2 3.8 copy-start.7
  423.9 255.9 %reduce-scatter.17.cloned.1.call-start = ((), (), s32[]{:S(2)}) async-start(), calls=%async_computation.17 | async-start | bytes 9437184 | tf_op jit(solution)/shard_map/reduce_scatter | solution.py:38
  477.9 5.9 copy-start.3
  495.8 7.1 copy-start.4
  516.3 7.1 copy-start.4
  536.6 7.1 copy-start.4
  557.1 7.1 copy-start.4
  569.2 7.0 copy-start.15
  576.2 1.9 copy-start.9
  576.2 1.9 copy-start.17
  578.1 1.9 copy-start.10
  578.1 1.9 copy-start.19
  584.7 158.1 %reduce-scatter.13.cloned.1.call-start = ((), (), s32[]{:S(2)}) async-start(), calls=%async_computation.13 | async-start | bytes 9437184 | tf_op jit(solution)/shard_map/reduce_scatter | solution.py:30
  594.2 228.6 %reduce-scatter.29.cloned.1.call-start = ((), (), s32[]{:S(2)}) async-start(), calls=%async_computation.23 | async-start | bytes 5013504 | tf_op jit(solution)/shard_map/reduce_scatter | solution.py:198
  604.3 297.9 %reduce-scatter.27.cloned.1.call-start = ((), (), s32[]{:S(2)}) async-start(), calls=%async_computation.22 | async-start | bytes 5013504 | tf_op jit(solution)/shard_map/reduce_scatter | solution.py:197
  614.5 349.1 %reduce-scatter.25.cloned.1.call-start = ((), (), s32[]{:S(2)}) async-start(), calls=%async_computation.21 | async-start | bytes 1253376 | tf_op jit(solution)/shard_map/reduce_scatter | solution.py:196
  619.8 405.0 %reduce-scatter.19.cloned.1.call-start = ((), (), s32[]{:S(2)}) async-start(), calls=%async_computation.18 | async-start | bytes 1253376 | tf_op jit(solution)/shard_map/reduce_scatter | solution.py:193
  625.2 460.8 %reduce-scatter.21.cloned.1.call-start = ((), (), s32[]{:S(2)}) async-start(), calls=%async_computation.19 | async-start | bytes 1253376 | tf_op jit(solution)/shard_map/reduce_scatter | solution.py:194
  630.0 517.1 %reduce-scatter.23.cloned.1.call-start = ((), (), s32[]{:S(2)}) async-start(), calls=%async_computation.20 | async-start | bytes 1253376 | tf_op jit(solution)/shard_map/reduce_scatter | solution.py:195
  635.5 4.7 copy-start.12
  635.5 44.3 %copy-start.21 = (f32[768]{0:T(1024)S(1)}, f32[768]{0:T(1024)}, u32[]{:S(2)}) copy-start(f32[768]{0:T(1024)} %copy-done.20) | copy-start | bytes 9220
  635.5 44.3 %copy-start.23 = (f32[1024]{0:T(1024)S(1)}, f32[1024]{0:T(1024)}, u32[]{:S(2)}) copy-start(f32[1024]{0:T(1024)} %copy-done.22) | copy-start | bytes 12292
  640.2 39.6 %copy-start.6 = (bf16[1024,768]{1,0:T(8,128)(2,1)S(1)}, bf16[1024,768]{1,0:T(8,128)(2,1)}, u32[]{:S(2)}) copy-start(bf16[1024,768]{1,0:T(8,128)(2,1)} %param.16) | copy-start | bytes 4718596
  640.2 80.1 %copy-start.25 = (f32[1024]{0:T(1024)S(1)}, f32[1024]{0:T(1024)}, u32[]{:S(2)}) copy-start(f32[1024]{0:T(1024)} %copy-done.24) | copy-start | bytes 12292
  742.8 404.4 %copy-start.1 = (bf16[768,1536]{1,0:T(8,128)(2,1)S(1)}, bf16[768,1536]{1,0:T(8,128)(2,1)}, u32[]{:S(2)}) copy-start(bf16[768,1536]{1,0:T(8,128)(2,1)} %param.24) | copy-start | bytes 7077892
  (4 other events, 2.6 us)
Sparse Core Ops, SparseCore 0:
  14.2 47.6 all-gather.4
  139.1 77.0 reduce-scatter.10
  222.3 44.9 all-gather.6
  268.7 44.9 all-gather.8
  339.1 77.0 reduce-scatter.14
  424.0 44.9 all-gather.10
  584.8 77.0 reduce-scatter.16
  664.3 78.4 reduce-scatter.12
  747.2 75.5 reduce-scatter.28
  827.6 74.5 reduce-scatter.26
  906.4 57.1 reduce-scatter.24
  967.6 57.0 reduce-scatter.18
  1028.9 57.0 reduce-scatter.20
  1090.1 57.0 reduce-scatter.22
where the time goes:
time: 1160 us; the launch traced here: 1150 us
  waiting for transfers between devices  736 us (63%)
  matrix products  177 us (15%)
  local copies, waits for them, and re-layouts  104 us (9%)
  blocking collectives  71.2 us (6%)
  other arithmetic  49.7 us (4%)
  between operations  14.4 us (1%)
    reduce_scatter x2, waiting for transfers between devices, sum_branch(): return lax.psum_scatter(values, 'tensor', scatter_dimension=0, tiled=True)  99 us
    all_gather x2, waiting for transfers between devices, gather_rows(): return lax.all_gather(values, 'tensor', axis=0, tiled=True)  85.5 us
    reduce_scatter x1, waiting for transfers between devices, shards(): lax.psum_scatter(grad_inner, 'dp', scatter_dimension=0, tiled=True)  79.4 us
    all_gather x2, waiting for transfers between devices, gather_grads(): return lax.all_gather(values, 'tensor', axis=0, tiled=True)  78.4 us
    reduce_scatter x2, waiting for transfers between devices, sum_back(): return lax.psum_scatter(values, 'tensor', scatter_dimension=0, tiled=True)  77.1 us
    reduce_scatter x1, waiting for transfers between devices, shards(): lax.psum_scatter(grad_outer, 'dp', scatter_dimension=1, tiled=True)  71.2 us
    reduce_scatter x1, waiting for transfers between devices, shards(): lax.psum_scatter(grad_output, 'dp', scatter_dimension=1, tiled=True)  61.3 us
    reduce_scatter x1, waiting for transfers between devices, shards(): lax.psum_scatter(grad_key, 'dp', scatter_dimension=0, tiled=True)  61.3 us
  transfers between devices with their start and end apart: 14, of which 13 were waited for; matrix products, arithmetic and copies ran while one was open for 8% of the time, Pallas kernels for 0%

commit v1 on v0

v1 whole, which is shorter than its diff:
```python
import functools

import jax
import jax.numpy as jnp
from jax import lax
from jax.experimental import pallas as pl
from jax.experimental.pallas import tpu as pltpu
from jax.sharding import PartitionSpec as P

HEAD_DIM = 64
BUCKETS = 32
EPS = 1e-6
MASKED = -1e9
GELU_C = 0.7978845608028654
VMEM_BYTES = 60 * 1024 * 1024
F32 = jnp.float32
BF16 = jnp.bfloat16


def dot(left, right):
    return lax.dot_general(left, right, (((1,), (0,)), ((), ())), preferred_element_type=F32)


def dot_t(left, right):
    return lax.dot_general(left, right, (((1,), (1,)), ((), ())), preferred_element_type=F32)


def bucket_of(offsets):
    distance = jnp.abs(offsets)
    far = jnp.full_like(distance, 8)
    for power in range(1, 8):
        far = far + (distance * distance >= 64 * 2**power).astype(jnp.int32)
    near = jnp.where(distance < 8, distance, far)
    return near + jnp.where(offsets > 0, 16, 0)


def bucket_indicator(seq):
    lane = lax.broadcasted_iota(jnp.int32, (BUCKETS, 2 * seq), 1)
    offsets = jnp.where(lane < seq, -lane, 2 * seq - lane)
    ids = lax.broadcasted_iota(jnp.int32, (BUCKETS, 2 * seq), 0)
    return (bucket_of(offsets) == ids).astype(F32)


def fill_bias(table_ref, bias_ref):
    heads, seq, _ = bias_ref.shape
    base = dot(table_ref[...], bucket_indicator(seq).astype(BF16))
    for h in range(heads):
        wide = jnp.broadcast_to(base[h : h + 1, :], (seq, 2 * seq))
        bias_ref[h] = pltpu.roll(wide, 0, 1, stride=1, stride_axis=0)[:, :seq]


def head_mask(columns, parity):
    lane = lax.broadcasted_iota(jnp.int32, columns.shape, 1)
    keep = (lane < HEAD_DIM) if parity == 0 else (lane >= HEAD_DIM)
    return jnp.where(keep, columns, jnp.zeros_like(columns))


def rms_rows(values, gain):
    return values * lax.rsqrt(jnp.mean(values * values, axis=-1, keepdims=True) + EPS) * gain


def rms_back(values, gain, grads):
    scale = lax.rsqrt(jnp.mean(values * values, axis=-1, keepdims=True) + EPS)
    scaled = grads * gain
    mean = jnp.mean(scaled * values, axis=-1, keepdims=True)
    back = scale * scaled - values * (scale * scale * scale * mean)
    return back, jnp.sum(grads * values * scale, axis=0, keepdims=True)


def attend(length, rows, wq_ref, wk_ref, wv_ref, bias_ref, q_ref, k_ref, v_ref, lse_ref):
    seq = rows.shape[0]
    heads = bias_ref.shape[0]
    query = dot(rows, wq_ref[...]).astype(BF16)
    keys = dot(rows, wk_ref[...]).astype(BF16)
    vals = dot(rows, wv_ref[...]).astype(BF16)
    q_ref[...] = query
    k_ref[...] = keys
    v_ref[...] = vals
    query_t = query.T
    vals_t = vals.T
    valid = lax.broadcasted_iota(jnp.int32, (seq, 1), 0) < length
    parts = []
    for h in range(heads):
        lo = (h // 2) * 2 * HEAD_DIM
        key_h = head_mask(keys[:, lo : lo + 2 * HEAD_DIM], h % 2)
        logits = dot(key_h, query_t[lo : lo + 2 * HEAD_DIM, :]) + bias_ref[h]
        logits = jnp.where(valid, logits, MASKED)
        peak = jnp.max(logits, axis=0, keepdims=True)
        terms = jnp.exp(logits - peak)
        total = jnp.sum(terms, axis=0, keepdims=True)
        probs = (terms * (1.0 / total)).astype(BF16)
        lse_ref[0, h : h + 1, :] = peak + jnp.log(total)
        parts.append(dot(vals_t[h * HEAD_DIM : (h + 1) * HEAD_DIM, :], probs))
    return jnp.concatenate(parts, axis=0).astype(BF16).T


def attn_first_kernel(
    len_ref, x_ref, gain_ref, cot_ref, perm_ref, wq_ref, wk_ref, wv_ref, table_ref,
    rows_ref, rows_t_ref, cot_t_ref, q_ref, k_ref, v_ref, ctx_ref, lse_ref, bias_ref,
):
    p = pl.program_id(0)

    @pl.when(p == 0)
    def _():
        fill_bias(table_ref, bias_ref)

    rows = rms_rows(x_ref[...].astype(F32), gain_ref[...]).astype(BF16)
    rows_ref[...] = rows
    rows_t_ref[...] = dot_t(perm_ref[...], rows).astype(BF16)
    cot_t_ref[...] = dot_t(perm_ref[...], cot_ref[...]).astype(BF16)
    ctx_ref[...] = attend(
        len_ref[p], rows, wq_ref, wk_ref, wv_ref, bias_ref, q_ref, k_ref, v_ref, lse_ref
    )


def attn_second_kernel(
    len_ref, x_ref, gain_ref, rows_ref, ctx_first_ref, perm_ref, wq_ref, wk_ref, wv_ref,
    wo_first_ref, wo_ref, table_ref,
    q_ref, k_ref, v_ref, ctx_ref, lse_ref, resid_ref, rows_two_ref, rows_two_t_ref, bias_ref,
):
    p = pl.program_id(0)

    @pl.when(p == 0)
    def _():
        fill_bias(table_ref, bias_ref)

    context = attend(
        len_ref[p], rows_ref[...], wq_ref, wk_ref, wv_ref, bias_ref, q_ref, k_ref, v_ref, lse_ref
    )
    ctx_ref[...] = context
    branch = dot(ctx_first_ref[...], wo_first_ref[...]) + dot(context, wo_ref[...])
    residual = x_ref[...].astype(F32) + branch
    resid_ref[...] = residual
    rows_two = rms_rows(residual, gain_ref[...]).astype(BF16)
    rows_two_ref[...] = rows_two
    rows_two_t_ref[...] = dot_t(perm_ref[...], rows_two).astype(BF16)


def ffn_block(
    rows_ref, rows_t_ref, cot_ref, cot_t_ref, wi_ref, wo_ref, ffn_ref, back_ref,
    send_ref, keep_ref, act_ref, grad_ref, chunk,
):
    count = rows_ref.shape[0] // chunk

    def step(i, carry):
        at = pl.ds(i * chunk, chunk)
        v = dot(rows_ref[at, :], wi_ref[...])
        grad_act = dot_t(cot_ref[at, :], wo_ref[...])
        square = v * v
        tanh = jnp.tanh(GELU_C * v * (1.0 + 0.044715 * square))
        half = 0.5 + 0.5 * tanh
        act = (v * half).astype(BF16)
        slope = half + (0.5 * GELU_C) * v * (1.0 - tanh * tanh) * (1.0 + 0.134145 * square)
        grad = (grad_act * slope).astype(BF16)
        act_ref[at, :] = act
        grad_ref[at, :] = grad
        ffn_ref[at, :] += dot(act, wo_ref[...])
        back_ref[at, :] += dot_t(grad, wi_ref[...])
        return carry

    lax.fori_loop(0, count, step, 0)
    half_rows = keep_ref.shape[1]
    part = half_rows // 2

    def weights(i, carry):
        at = pl.ds(i * part, part)
        after = pl.ds(half_rows + i * part, part)
        keep_ref[0, at, :] = dot(rows_t_ref[at, :], grad_ref[...]).astype(BF16)
        keep_ref[1, at, :] = dot(cot_t_ref[at, :], act_ref[...]).astype(BF16)
        send_ref[0, at, :] = dot(rows_t_ref[after, :], grad_ref[...]).astype(BF16)
        send_ref[1, at, :] = dot(cot_t_ref[after, :], act_ref[...]).astype(BF16)
        return carry

    lax.fori_loop(0, 2, weights, 0)


def ffn_first_kernel(
    rows_ref, rows_t_ref, cot_ref, cot_t_ref, wi_ref, wo_ref,
    ffn_ref, back_ref, send_ref, keep_ref, act_ref, grad_ref, *, chunk,
):
    @pl.when(pl.program_id(0) == 0)
    def _():
        ffn_ref[...] = jnp.zeros_like(ffn_ref)
        back_ref[...] = jnp.zeros_like(back_ref)

    ffn_block(
        rows_ref, rows_t_ref, cot_ref, cot_t_ref, wi_ref, wo_ref, ffn_ref, back_ref,
        send_ref, keep_ref, act_ref, grad_ref, chunk,
    )


def ffn_second_kernel(
    rows_ref, rows_t_ref, cot_ref, cot_t_ref, wi_ref, wo_ref, ffn_in_ref, back_in_ref,
    resid_ref, gain_ref, perm_ref,
    layer_ref, grad_resid_ref, grad_attn_ref, grad_attn_t_ref, gain_grad_ref, send_ref, keep_ref,
    ffn_ref, back_ref, act_ref, grad_ref, *, chunk,
):
    @pl.when(pl.program_id(0) == 0)
    def _():
        ffn_ref[...] = ffn_in_ref[...]
        back_ref[...] = back_in_ref[...]

    ffn_block(
        rows_ref, rows_t_ref, cot_ref, cot_t_ref, wi_ref, wo_ref, ffn_ref, back_ref,
        send_ref, keep_ref, act_ref, grad_ref, chunk,
    )

    @pl.when(pl.program_id(0) == pl.num_programs(0) - 1)
    def _():
        gain_grad_ref[...] = jnp.zeros_like(gain_grad_ref)

        def step(i, carry):
            at = pl.ds(i * chunk, chunk)
            residual = resid_ref[at, :]
            layer_ref[at, :] = (residual + ffn_ref[at, :]).astype(BF16)
            back, gain_part = rms_back(residual, gain_ref[...], back_ref[at, :])
            gain_grad_ref[...] += gain_part
            grad_resid = cot_ref[at, :].astype(F32) + back
            grad_resid_ref[at, :] = grad_resid
            grad_attn_ref[at, :] = grad_resid.astype(BF16)
            return carry

        lax.fori_loop(0, rows_ref.shape[0] // chunk, step, 0)
        half_rows = perm_ref.shape[0] // 2

        def turn(i, carry):
            at = pl.ds(i * half_rows, half_rows)
            grad_attn_t_ref[at, :] = dot_t(perm_ref[at, :], grad_attn_ref[...]).astype(BF16)
            return carry

        lax.fori_loop(0, 2, turn, 0)


def attn_back_kernel(
    len_ref, grad_attn_ref, wo_ref, q_ref, k_ref, v_ref, ctx_ref, lse_ref, table_ref,
    rows_t_ref, grad_attn_t_ref,
    dqkv_ref, send_ref, keep_ref, table_grad_ref, bias_ref, sums_ref, ctx_all_ref, *, seq,
):
    p = pl.program_id(0)
    heads = bias_ref.shape[0]
    width = heads * HEAD_DIM

    @pl.when(p == 0)
    def _():
        fill_bias(table_ref, bias_ref)
        sums_ref[...] = jnp.zeros_like(sums_ref)

    here = pl.ds(p * seq, seq)
    ctx_all_ref[here, :] = ctx_ref[...]
    grad_ctx = dot_t(grad_attn_ref[...], wo_ref[...]).astype(BF16)
    grad_ctx_t = grad_ctx.T
    query = q_ref[...]
    query_t = query.T
    keys = k_ref[...]
    keys_t = keys.T
    vals = v_ref[...]
    valid = lax.broadcasted_iota(jnp.int32, (seq, 1), 0) < len_ref[p]
    first_head = lax.broadcasted_iota(jnp.int32, (seq, 2 * HEAD_DIM), 1) < HEAD_DIM
    dq_parts, dk_parts, dv_parts = [], [], []
    for pair in range(heads // 2):
        lo = pair * 2 * HEAD_DIM
        both = slice(lo, lo + 2 * HEAD_DIM)
        for parity in range(2):
            h = 2 * pair + parity
            own = slice(h * HEAD_DIM, (h + 1) * HEAD_DIM)
            logits = dot(head_mask(keys[:, both], parity), query_t[both, :]) + bias_ref[h]
            probs = jnp.where(valid, jnp.exp(logits - lse_ref[0, h : h + 1, :]), 0.0)
            grad_probs = dot(head_mask(vals[:, both], parity), grad_ctx_t[both, :])
            mixed = jnp.sum(probs * grad_probs, axis=0, keepdims=True)
            grads = (probs * (grad_probs - mixed)).astype(BF16)
            sums_ref[h] += grads.astype(F32)
            dq_parts.append(dot(keys_t[own, :], grads))
            dk_parts.append(dot(grads, query[:, both]))
            dv_parts.append(dot(probs.astype(BF16), grad_ctx[:, both]))
    dq = jnp.concatenate(dq_parts, axis=0).astype(BF16).T
    dqkv_ref[here, :width] = dq
    for pair in range(heads // 2):
        lo = pair * 2 * HEAD_DIM
        dk = jnp.where(first_head, dk_parts[2 * pair], dk_parts[2 * pair + 1])
        dv = jnp.where(first_head, dv_parts[2 * pair], dv_parts[2 * pair + 1])
        dqkv_ref[here, width + lo : width + lo + 2 * HEAD_DIM] = dk.astype(BF16)
        dqkv_ref[here, 2 * width + lo : 2 * width + lo + 2 * HEAD_DIM] = dv.astype(BF16)

    @pl.when(p == pl.num_programs(0) - 1)
    def _():
        half_rows = keep_ref.shape[0]
        part = half_rows // 2

        def weights(i, carry):
            at = pl.ds(i * part, part)
            after = pl.ds(half_rows + i * part, part)
            keep_ref[at, : 3 * width] = dot(rows_t_ref[at, :], dqkv_ref[...]).astype(BF16)
            keep_ref[at, 3 * width :] = dot(grad_attn_t_ref[at, :], ctx_all_ref[...]).astype(BF16)
            send_ref[at, : 3 * width] = dot(rows_t_ref[after, :], dqkv_ref[...]).astype(BF16)
            send_ref[at, 3 * width :] = dot(grad_attn_t_ref[after, :], ctx_all_ref[...]).astype(BF16)
            return carry

        lax.fori_loop(0, 2, weights, 0)
        indicator = bucket_indicator(seq)
        lane = lax.broadcasted_iota(jnp.int32, table_grad_ref.shape, 1)
        table_grad = jnp.zeros_like(table_grad_ref)
        for h in range(heads):
            folded = jnp.zeros((8, 2 * seq), F32)
            for a in range(0, seq, 8):
                wide = jnp.concatenate([sums_ref[h, a : a + 8, :], jnp.zeros((8, seq), F32)], axis=1)
                folded = folded + (pltpu.roll(wide, 2 * seq - a, 1) if a else wide)
            diagonals = folded[0:1, :]
            for b in range(1, 8):
                diagonals = diagonals + pltpu.roll(folded[b : b + 1, :], 2 * seq - b, 1)
            column = jnp.sum(indicator * diagonals, axis=1, keepdims=True)
            table_grad = jnp.where(lane == h, column, table_grad)
        table_grad_ref[...] = table_grad


def input_back_kernel(
    x_ref, gain_ref, grad_resid_ref, d_first_ref, d_second_ref,
    wq_first_ref, wk_first_ref, wv_first_ref, wq_ref, wk_ref, wv_ref,
    grad_input_ref, gain_grad_ref,
):
    @pl.when(pl.program_id(0) == 0)
    def _():
        gain_grad_ref[...] = jnp.zeros_like(gain_grad_ref)

    width = wq_ref.shape[1]
    total = None
    for d_ref, refs in (
        (d_first_ref, (wq_first_ref, wk_first_ref, wv_first_ref)),
        (d_second_ref, (wq_ref, wk_ref, wv_ref)),
    ):
        for n, ref in enumerate(refs):
            term = dot_t(d_ref[:, n * width : (n + 1) * width], ref[...])
            total = term if total is None else total + term
    back, gain_part = rms_back(x_ref[...].astype(F32), gain_ref[...], total)
    grad_input_ref[...] = grad_resid_ref[...] + back
    gain_grad_ref[...] += gain_part


def whole_spec(array_shape):
    return pl.BlockSpec(array_shape, lambda i: (0,) * len(array_shape), pipeline_mode=pl.Buffered(1))


def call(kernel, grid, ins, outs, scratch, cost, name):
    arrays = [a for a, _ in ins]
    return pl.pallas_call(
        kernel,
        grid=grid,
        in_specs=[s for _, s in ins],
        out_specs=[s for _, _, s in outs],
        out_shape=[jax.ShapeDtypeStruct(s, d) for s, d, _ in outs],
        scratch_shapes=scratch,
        compiler_params=pltpu.CompilerParams(
            dimension_semantics=("arbitrary",), vmem_limit_bytes=VMEM_BYTES
        ),
        cost_estimate=pl.CostEstimate(flops=cost, bytes_accessed=cost // 1000, transcendentals=0),
        name=name,
    )(*arrays)


def shards(
    inputs, gain_attn, w_query, w_key, w_value, w_output, relative_bias_table,
    gain_ffn, w_inner, w_outer, lengths, cotangent, *, dp, tp,
):
    rows_n, width = inputs.shape
    passages = lengths.shape[0] // tp
    seq = rows_n // passages
    cols = w_query.shape[1]
    heads = cols // HEAD_DIM
    hidden = w_inner.shape[1]
    me = lax.axis_index("dp")
    side = lax.axis_index("tensor")
    core = me % 2
    rest = dp // 4

    def across(value, distance):
        return lax.ppermute(value, "dp", [(i, i ^ distance) for i in range(dp)])

    def beside(value):
        return lax.ppermute(value, "tensor", [(i, tp - 1 - i) for i in range(tp)])

    def fetch(weight):
        half = weight.shape[0] // 2
        mine = lax.dynamic_slice_in_dim(weight, core * half, half, 0)
        got = beside(mine)
        other = across(got, 1)
        return jnp.where(
            core == 0,
            jnp.concatenate([got, other], axis=0),
            jnp.concatenate([other, got], axis=0),
        )

    table = jnp.pad(relative_bias_table.T, ((0, 16 - heads), (0, 0)))
    table_far = beside(table)
    qkv_far = fetch(jnp.concatenate([w_query, w_key, w_value], axis=1))
    wq_far, wk_far, wv_far = (qkv_far[:, n * cols : (n + 1) * cols] for n in range(3))
    wo_far = fetch(w_output)
    wi_far = fetch(w_inner)
    wout_far = fetch(w_outer)

    lens = lax.dynamic_slice_in_dim(lengths, side * passages, passages, 0)
    gain_one = gain_attn.astype(F32).reshape(1, width)
    gain_two = gain_ffn.astype(F32).reshape(1, width)

    block = width // dp
    index = lax.broadcasted_iota(jnp.int32, (width, width), 0)
    source = lax.broadcasted_iota(jnp.int32, (width, width), 1)
    rel = index // block
    rel_dp = (rel % rest) * 4 + ((rel // rest) % 2) * 2 + rel // (2 * rest)
    perm = (source == (rel_dp ^ me) * block + index % block).astype(BF16)

    smem = pl.BlockSpec(memory_space=pltpu.SMEM)
    by_passage = lambda c: pl.BlockSpec((seq, c), lambda p: (p, 0))
    by_passage_t = pl.BlockSpec((width, seq), lambda p: (0, p))
    lse_spec = pl.BlockSpec((1, 8, seq), lambda p: (p, 0, 0))
    weight_spec = whole_spec((width, cols))
    table_spec = whole_spec((16, BUCKETS))
    gain_spec = whole_spec((1, width))
    perm_spec = whole_spec((width, width))
    wo_spec = whole_spec((cols, width))
    qkv_outs = [((rows_n, cols), BF16, by_passage(cols))] * 4 + [((passages, 8, seq), F32, lse_spec)]
    bias_scratch = pltpu.VMEM((heads, seq, seq), F32)
    attn_cost = 2 * rows_n * (width * 3 * cols + seq * 4 * cols)

    rows_one, rows_one_t, cot_t, q_near, k_near, v_near, ctx_near, lse_near = call(
        attn_first_kernel, (passages,),
        [(lens, smem), (inputs, by_passage(width)), (gain_one, gain_spec), (cotangent, by_passage(width)),
         (perm, perm_spec), (w_query, weight_spec), (w_key, weight_spec), (w_value, weight_spec),
         (table, table_spec)],
        [((rows_n, width), BF16, by_passage(width)), ((width, rows_n), BF16, by_passage_t),
         ((width, rows_n), BF16, by_passage_t)] + qkv_outs,
        [bias_scratch], attn_cost, "attn_first",
    )
    q_far, k_far, v_far, ctx_far, lse_far, residual, rows_two, rows_two_t = call(
        attn_second_kernel, (passages,),
        [(lens, smem), (inputs, by_passage(width)), (gain_two, gain_spec), (rows_one, by_passage(width)),
         (ctx_near, by_passage(cols)), (perm, perm_spec), (wq_far, weight_spec), (wk_far, weight_spec),
         (wv_far, weight_spec), (w_output, wo_spec), (wo_far, wo_spec), (table_far, table_spec)],
        qkv_outs + [((rows_n, width), F32, by_passage(width)), ((rows_n, width), BF16, by_passage(width)),
                    ((width, rows_n), BF16, by_passage_t)],
        [bias_scratch], attn_cost, "attn_second",
    )

    block_hidden = 512 if hidden % 512 == 0 else hidden
    steps = hidden // block_hidden
    chunk = min(256, rows_n)
    full = whole_spec((rows_n, width))
    full_t = whole_spec((width, rows_n))
    wi_spec = pl.BlockSpec((width, block_hidden), lambda i: (0, i))
    wout_spec = pl.BlockSpec((block_hidden, width), lambda i: (i, 0))
    grad_spec = pl.BlockSpec((2, width // 2, block_hidden), lambda i: (0, 0, i))
    grad_out = ((2, width // 2, hidden), BF16, grad_spec)
    acc_out = ((rows_n, width), F32, full)
    hidden_scratch = [pltpu.VMEM((rows_n, block_hidden), BF16)] * 2
    ffn_cost = 12 * rows_n * width * hidden

    ffn_near, back_near, fg_send_near, fg_keep_near = call(
        functools.partial(ffn_first_kernel, chunk=chunk), (steps,),
        [(rows_two, full), (rows_two_t, full_t), (cotangent, full), (cot_t, full_t),
         (w_inner, wi_spec), (w_outer, wout_spec)],
        [acc_out, acc_out, grad_out, grad_out],
        hidden_scratch, ffn_cost, "ffn_first",
    )
    layer_out, grad_residual, grad_attn, grad_attn_t, gain_two_part, fg_send_far, fg_keep_far = call(
        functools.partial(ffn_second_kernel, chunk=chunk), (steps,),
        [(rows_two, full), (rows_two_t, full_t), (cotangent, full), (cot_t, full_t),
         (wi_far, wi_spec), (wout_far, wout_spec), (ffn_near, full), (back_near, full),
         (residual, full), (gain_two, gain_spec), (perm, perm_spec)],
        [((rows_n, width), BF16, full), acc_out, ((rows_n, width), BF16, full),
         ((width, rows_n), BF16, full_t), ((1, width), F32, gain_spec), grad_out, grad_out],
        [pltpu.VMEM((rows_n, width), F32)] * 2 + hidden_scratch, ffn_cost, "ffn_second",
    )

    def attn_back(wo, q, k, v, ctx, lse, tab, name):
        half_spec = whole_spec((width // 2, 4 * cols))
        half_out = ((width // 2, 4 * cols), BF16, half_spec)
        return call(
            functools.partial(attn_back_kernel, seq=seq), (passages,),
            [(lens, smem), (grad_attn, by_passage(width)), (wo, wo_spec), (q, by_passage(cols)),
             (k, by_passage(cols)), (v, by_passage(cols)), (ctx, by_passage(cols)), (lse, lse_spec),
             (tab, table_spec), (rows_one_t, full_t), (grad_attn_t, full_t)],
            [((rows_n, 3 * cols), BF16, whole_spec((rows_n, 3 * cols))), half_out, half_out,
             ((BUCKETS, 128), F32, whole_spec((BUCKETS, 128)))],
            [bias_scratch, pltpu.VMEM((heads, seq, seq), F32), pltpu.VMEM((rows_n, cols), BF16)],
            2 * rows_n * cols * (5 * width + 5 * seq), name,
        )

    d_far, ag_send_far, ag_keep_far, table_part_far = attn_back(
        wo_far, q_far, k_far, v_far, ctx_far, lse_far, table_far, "attn_back_far"
    )
    d_near, ag_send_near, ag_keep_near, table_part_near = attn_back(
        w_output, q_near, k_near, v_near, ctx_near, lse_near, table, "attn_back_near"
    )
    grad_input, gain_one_part = call(
        input_back_kernel, (passages,),
        [(inputs, by_passage(width)), (gain_one, gain_spec), (grad_residual, by_passage(width)),
         (d_near, by_passage(3 * cols)), (d_far, by_passage(3 * cols)),
         (w_query, weight_spec), (w_key, weight_spec), (w_value, weight_spec),
         (wq_far, weight_spec), (wk_far, weight_spec), (wv_far, weight_spec)],
        [((rows_n, width), F32, by_passage(width)), ((1, width), F32, gain_spec)],
        [], 12 * rows_n * width * cols, "input_back",
    )

    def plus(left, right):
        return (left.astype(F32) + right.astype(F32)).astype(BF16)

    def reduce_weights(send_near, keep_near, send_far, keep_far):
        near = plus(keep_near, across(send_near, 1))
        far = plus(keep_far, across(send_far, 1))
        mine = plus(near, beside(far))
        lead, tail = mine.shape[:-2], mine.shape[-1]
        halves = mine.reshape(lead + (2, mine.shape[-2] // 2, tail))
        mine = plus(halves[..., 0, :, :], across(halves[..., 1, :, :], 2))
        size, scale = rest, 4
        while size > 1:
            ways = min(4, size)
            rel_parts = mine.reshape(lead + (ways, mine.shape[-2] // ways, tail))
            low = scale * (size // ways)
            total = rel_parts[..., 0, :, :].astype(F32)
            for w in range(1, ways):
                total = total + across(rel_parts[..., w, :, :], w * low).astype(F32)
            size //= ways
            mine = total.astype(BF16) if size > 1 else total
        return mine.astype(F32)

    ffn_grads = reduce_weights(fg_send_near, fg_keep_near, fg_send_far, fg_keep_far)
    attn_grads = reduce_weights(ag_send_near, ag_keep_near, ag_send_far, ag_keep_far)
    grad_inner = ffn_grads[0]
    grad_outer = ffn_grads[1].T
    grad_query, grad_key, grad_value = (attn_grads[:, n * cols : (n + 1) * cols] for n in range(3))
    grad_output = attn_grads[:, 3 * cols :].T

    table_sum = table_part_near[:, :heads] + beside(table_part_far[:, :heads])
    small = jnp.concatenate([gain_one_part, gain_two_part], axis=1)
    small = small + beside(small)
    both = jnp.concatenate([small, table_sum.reshape(1, -1)], axis=1)
    distance = 1
    while distance < dp:
        both = both + across(both, distance)
        distance *= 2
    grad_gain_one = both[0, :width]
    grad_gain_two = both[0, width : 2 * width]
    grad_table = both[0, 2 * width :].reshape(BUCKETS, heads)
    return (
        layer_out, grad_input, grad_gain_one, grad_query, grad_key, grad_value, grad_output,
        grad_table, grad_gain_two, grad_inner, grad_outer,
    )


def solution(mesh):
    both = ("dp", "tensor")
    in_specs = (
        P(both, None), P(), P(None, "tensor"), P(None, "tensor"), P(None, "tensor"), P("tensor", None),
        P(None, "tensor"), P(), P(None, "tensor"), P("tensor", None), P("dp"), P(both, None),
    )
    out_specs = (
        P(both, None), P(both, None), P(), P("dp", "tensor"), P("dp", "tensor"), P("dp", "tensor"),
        P("tensor", "dp"), P(None, "tensor"), P(), P("dp", "tensor"), P("tensor", "dp"),
    )
    body = functools.partial(shards, dp=mesh.shape["dp"], tp=mesh.shape["tensor"])
    return jax.shard_map(body, mesh=mesh, in_specs=in_specs, out_specs=out_specs, check_vma=False)
```

time: 1160 us -> 386 us (0.33)
  waiting for transfers between devices: 736 us -> 154 us
  matrix products: 177 us -> 0 us
  Pallas kernels: 0 us -> 150 us
  local copies, waits for them, and re-layouts: 104 us -> 19.8 us
  blocking collectives: 71.2 us -> 0 us
  starting transfers between devices: 0.92 us -> 29.4 us
  other arithmetic: 49.7 us -> 31.1 us
  between operations: 14.4 us -> 0.95 us
    reduce_scatter x10 -> x0, waiting for transfers between devices: 572 us -> none  [the longest x2 99 us: sum_branch(): return lax.psum_scatter(values, 'tensor', scatter_dimension=0, tiled=True)]
    dot_general x48 -> x0, matrix products: 177 us -> none  [the longest x6 39.1 us: matmul(): return jnp.dot(left, right, preferred_element_type=jnp.float32)]
    all_gather x4 -> x0, waiting for transfers between devices: 164 us -> none  [the longest x2 85.5 us: gather_rows(): return lax.all_gather(values, 'tensor', axis=0, tiled=True)]
    ppermute x0 -> x29, waiting for transfers between devices: none -> 154 us  [the longest x9 104 us: beside(): return lax.ppermute(value, 'tensor', [(i, tp - 1 - i) for i in range(tp)])]
    pallas_call x0 -> x7, Pallas kernels: none -> 150 us  [call(): pl.pallas_call(kernel, grid=grid, in_specs=[s for _, s in ins], out_specs...]
    psum x2 -> x0, blocking collectives: 71.2 us -> none  [the longest x1 37.5 us: shards(): lax.psum((grad_gain_one, grad_gain_two), ('dp', 'tensor'))]
    dynamic_update_slice x20 -> x0, local copies, waits for them, and re-layouts: 33.9 us -> none  [the longest x8 17.6 us: shards(): lax.map(attend_back, (query_five, key_five, value_five, key_mask, log_tot...]
    reduce_sum x13 -> x0, other arithmetic: 31.3 us -> none  [the longest x4 12.3 us: attend_back(): bias_part = jnp.sum(grad_low.astype(jnp.float32), axis=0)]
  transfers between devices with their start and end apart: 14 -> 29, of which waited for: 13 -> 12; matrix products, arithmetic and copies ran while one was open for 8% -> 11% of each run, Pallas kernels for 0% -> 30%
where the time goes in v1:
time: 386 us
  waiting for transfers between devices  154 us (40%)
  Pallas kernels  150 us (39%)
  other arithmetic  31.1 us (8%)
  starting transfers between devices  29.4 us (8%)
  local copies, waits for them, and re-layouts  19.8 us (5%)
    pallas_call x7, Pallas kernels, call(): pl.pallas_call(kernel, grid=grid, in_specs=[s for _, s in ins], out_specs...  150 us
    ppermute x9, waiting for transfers between devices, beside(): return lax.ppermute(value, 'tensor', [(i, tp - 1 - i) for i in range(tp)])  104 us
    ppermute x20, waiting for transfers between devices, across(): return lax.ppermute(value, 'dp', [(i, i ^ distance) for i in range(dp)])  50.4 us
    ppermute x20, starting transfers between devices, across(): return lax.ppermute(value, 'dp', [(i, i ^ distance) for i in range(dp)])  18.1 us
    convert_element_type x6, other arithmetic, plus(): return (left.astype(F32) + right.astype(F32)).astype(BF16)  13.2 us
    ppermute x9, starting transfers between devices, beside(): return lax.ppermute(value, 'tensor', [(i, tp - 1 - i) for i in range(tp)])  11.3 us
    select_n x4, other arithmetic, fetch(): jnp.where(core == 0, jnp.concatenate([got, other], axis=0), jnp.concatena...  9.42 us
  transfers between devices with their start and end apart: 29, of which 12 were waited for; matrix products, arithmetic and copies ran while one was open for 11% of the time, Pallas kernels for 30%

profile of v1, /device:TPU:0, one launch (start us, length us, event | category | flops | bytes accessed | tf_op | source)
XLA Modules:
  0.0 385.5 jit_solution(1364171500895278564)
XLA Ops:
  0.7 2.3 fusion.19
  3.0 2.9 collective-permute-start
  6.8 2.0 collective-permute-start.2
  9.0 2.4 constant_dynamic-slice_fusion.1
  11.3 2.0 collective-permute-start.5
  13.4 19.8 %collective-permute-done.2 = bf16[192,768]{1,0:T(8,128)(2,1)} collective-permute-done((bf16[192,768]{1,0:T(8,128)(2,1)}, bf16[192,768]{1,0:T(8,128)(2,1)}, u32[]{:S(2)}, u32[]{:S(2)}) %collective-permute-start.2) | collective-permute-done | bytes 294944 | tf_op jit(solution)/shard_map/ppermute | solution.py:378
  33.6 3.1 fusion.17.perm_ref
  37.9 1.2 dynamic_slice.15.len_ref
  39.2 17.3 %attn_first.1 = (bf16[1024,768]{1,0:T(8,128)(2,1)}, bf16[768,1024]{1,0:T(8,128)(2,1)}, bf16[768,1024]{1,0:T(8,128)(2,1)}, bf16[1024,384]{1,0:T(8,128)(2,1)}, bf1...) custom-call(s32[4]{0:T(128)} %dynamic_slice.15.len_ref, ...), custom_call_target="tpu_custom_call" | custom-call | flops 2617245696 | bytes 2617245 | tf_op jit(solution)/shard_map/attn_first/pallas_call | solution.py:344
  56.5 2.2 maximum_select_fusion.3.wo_ref
  58.7 24.0 %collective-permute-done.5 = bf16[384,1536]{1,0:T(8,128)(2,1)S(1)} collective-permute-done((bf16[384,1536]{1,0:T(8,128)(2,1)}, bf16[384,1536]{1,0:T(8,128)(2,1)S(1)}, u32[]{:S(2)}, u32[]{:S(2)}) %collective-permute-start.5) | collective-permute-done | bytes 1179680 | tf_op jit(solution)/shard_map/ppermute | solution.py:378
  82.7 2.4 maximum_select_fusion.2
  85.2 1.3 fusion.29
  87.1 20.0 %attn_second.1 = (bf16[1024,384]{1,0:T(8,128)(2,1)}, bf16[1024,384]{1,0:T(8,128)(2,1)}, bf16[1024,384]{1,0:T(8,128)(2,1)}, bf16[1024,384]{1,0:T(8,128)(2,1)}, f3...) custom-call(s32[4]{0:T(128)} %dynamic_slice.15.len_ref, ...), custom_call_target="tpu_custom_call" | custom-call | flops 2617245696 | bytes 2617245 | tf_op jit(solution)/shard_map/attn_second/pallas_call | solution.py:344
  107.1 26.2 %ffn_first.1 = (f32[1024,768]{1,0:T(8,128)}, f32[1024,768]{1,0:T(8,128)}, bf16[2,384,1536]{2,1,0:T(8,128)(2,1)}, bf16[2,384,1536]{2,1,0:T(8,128)(2,1)}) custom-call(bf16[1024,768]{1,0:T(8,128)(2,1)} %get-tuple-element.50.rows_ref, bf16[768,1024]{1,0:T(8,128)(2,1)} %get-tuple-element.51.rows_t_ref, bf16[1024,768]{1,0:T(8,128)(2,1)} %cot_ref.5, ...), custom_call_target="tpu_custom_call" | custom-call | flops 14495514624 | bytes 14495514 | tf_op jit(solution)/shard_map/ffn_first/pallas_call | solution.py:344
  133.3 1.8 maximum_select_fusion.1.wo_ref
  135.1 3.0 maximum_select_fusion.wi_ref
  138.1 33.6 %ffn_second.1 = (bf16[1024,768]{1,0:T(8,128)(2,1)}, f32[1024,768]{1,0:T(8,128)}, bf16[1024,768]{1,0:T(8,128)(2,1)}, bf16[768,1024]{1,0:T(8,128)(2,1)}, f32[1,768...) custom-call(bf16[1024,768]{1,0:T(8,128)(2,1)} %get-tuple-element.50.rows_ref, ...), custom_call_target="tpu_custom_call" | custom-call | flops 14495514624 | bytes 14495514 | tf_op jit(solution)/shard_map/ffn_second/pallas_call | solution.py:344
  172.2 21.1 %attn_back_far.1 = (bf16[1024,1152]{1,0:T(8,128)(2,1)}, bf16[384,1536]{1,0:T(8,128)(2,1)}, bf16[384,1536]{1,0:T(8,128)(2,1)}, f32[32,128]{1,0:T(8,128)}) custom-call(s32[4]{0:T(128)} %dynamic_slice.15.len_ref, bf16[1024,768]{1,0:T(8,128)(2,1)} %get-tuple-element.58.grad_attn_ref, bf16[384,768]{1,0:T(8,128)(2,1)} %maximum_select_fusion.3.wo_ref, ...), custom_call_target="tpu_custom_call" | custom-call | flops 4026531840 | bytes 4026531 | tf_op jit(solution)/shard_map/attn_back_far/pallas_call | solution.py:344
  193.8 1.7 collective-permute-start.10
  195.6 21.4 %attn_back_near.1 = (bf16[1024,1152]{1,0:T(8,128)(2,1)}, bf16[384,1536]{1,0:T(8,128)(2,1)}, bf16[384,1536]{1,0:T(8,128)(2,1)}, f32[32,128]{1,0:T(8,128)}) custom-call(s32[4]{0:T(128)} %dynamic_slice.15.len_ref, bf16[1024,768]{1,0:T(8,128)(2,1)} %get-tuple-element.58.grad_attn_ref, bf16[384,768]{1,0:T(8,128)(2,1)} %wo_ref.3, ...), custom_call_target="tpu_custom_call" | custom-call | flops 4026531840 | bytes 4026531 | tf_op jit(solution)/shard_map/attn_back_near/pallas_call | solution.py:344
  217.0 1.4 copy-done
  218.4 3.1 add_convert_fusion.1
  222.9 1.5 add_convert_fusion.4
  224.4 1.8 collective-permute-start.17
  226.2 10.6 %input_back.1 = (f32[1024,768]{1,0:T(8,128)}, f32[1,768]{1,0:T(1,128)}) custom-call(bf16[1024,768]{1,0:T(8,128)(2,1)} %x_ref.5, f32[1,768]{1,0:T(1,128)} %reshape.69.gain_ref, f32[1024,768]{1,0:T(8,128)} %get-tuple-element.57.grad_resid_ref, bf16[1024,1152]{1,0:T(8,128)(2,1)} %get-tuple-element.65.d_first_ref, ...), custom_call_target="tpu_custom_call" | custom-call | flops 3623878656 | bytes 3623878 | tf_op jit(solution)/shard_map/input_back/pallas_call | solution.py:344
  236.9 1.3 constant_dynamic-update-slice_fusion.1
  240.7 60.0 %collective-permute-done.9 = f32[1,1536]{1,0:T(1,128)} collective-permute-done((f32[1,1536]{1,0:T(1,128)}, f32[1,1536]{1,0:T(1,128)}, u32[]{:S(2)}, u32[]{:S(2)}) %collective-permute-start.9) | collective-permute-done | bytes 6176 | tf_op jit(solution)/shard_map/ppermute | solution.py:378
  304.0 1.6 collective-permute-start.12
  305.6 2.1 collective-permute-done.12
  307.7 1.6 collective-permute-start.13
  309.4 2.1 collective-permute-done.13
  311.4 2.7 collective-permute-start.14
  314.1 1.9 collective-permute-done.14
  316.1 2.6 add_convert_fusion.3
  319.5 1.5 collective-permute-start.18
  321.1 3.3 add_convert_fusion
  328.0 1.3 slice_reduce_fusion
  329.3 6.8 %collective-permute-done.18 = bf16[192,1536]{1,0:T(8,128)(2,1)} collective-permute-done((bf16[192,1536]{1,0:T(8,128)(2,1)}, bf16[192,1536]{1,0:T(8,128)(2,1)}, u32[]{:S(2)}, u32[]{:S(2)}) %collective-permute-start.18) | collective-permute-done | bytes 589856 | tf_op jit(solution)/shard_map/ppermute | solution.py:375
  337.3 1.6 collective-permute-start.19
  339.0 2.5 collective-permute-start.21
  341.6 15.5 %collective-permute-done.25 = bf16[2,192,1536]{2,1,0:T(8,128)(2,1)} collective-permute-done((bf16[2,192,1536]{2,1,0:T(8,128)(2,1)}, bf16[2,192,1536]{2,1,0:T(8,128)(2,1)}, u32[]{:S(2)}, u32[]{:S(2)}) %collective-permute-start.25) | collective-permute-done | bytes 1179680 | tf_op jit(solution)/shard_map/ppermute | solution.py:375
  357.1 1.5 fusion.15
  358.7 1.6 collective-permute-start.26
  360.3 2.5 collective-permute-start.28
  363.7 6.3 %collective-permute-done.26 = bf16[2,48,1536]{2,1,0:T(8,128)(2,1)S(1)} collective-permute-done((bf16[2,48,1536]{2,1,0:T(8,128)(2,1)S(1)}, bf16[2,48,1536]{2,1,0:T(8,128)(2,1)S(1)}, u32[]{:S(2)}, u32[]{:S(2)}) %collective-permute-start.26) | collective-permute-done | bytes 294944 | tf_op jit(solution)/shard_map/ppermute | solution.py:375
  370.0 5.0 %collective-permute-done.28 = bf16[2,48,1536]{2,1,0:T(8,128)(2,1)S(1)} collective-permute-done((bf16[2,48,1536]{2,1,0:T(8,128)(2,1)S(1)}, bf16[2,48,1536]{2,1,0:T(8,128)(2,1)S(1)}, u32[]{:S(2)}, u32[]{:S(2)}) %collective-permute-start.28) | collective-permute-done | bytes 294944 | tf_op jit(solution)/shard_map/ppermute | solution.py:375
  375.0 9.6 %collective-permute-done.27 = bf16[2,48,1536]{2,1,0:T(8,128)(2,1)S(1)} collective-permute-done((bf16[2,48,1536]{2,1,0:T(8,128)(2,1)S(1)}, bf16[2,48,1536]{2,1,0:T(8,128)(2,1)S(1)}, u32[]{:S(2)}, u32[]{:S(2)}) %collective-permute-start.27) | collective-permute-done | bytes 294944 | tf_op jit(solution)/shard_map/ppermute | solution.py:375
  (92 shorter events, 19.6 us)
Async XLA Ops:
  0.6 5.3 %copy-start.11 = (bf16[32,6]{0,1:T(8,128)(2,1)S(1)}, bf16[32,6]{0,1:T(8,128)(2,1)}, u32[]{:S(2)}) copy-start(bf16[32,6]{0,1:T(8,128)(2,1)} %param.18) | copy-start | bytes 1156
  0.7 5.4 %copy-start.5 = (bf16[384,768]{1,0:T(8,128)(2,1)S(1)}, bf16[384,768]{1,0:T(8,128)(2,1)}, u32[]{:S(2)}) copy-start(bf16[384,768]{1,0:T(8,128)(2,1)} %wo_ref.3) | copy-start | bytes 1769476
  0.7 8.1 %copy-start.4 = (bf16[1536,768]{1,0:T(8,128)(2,1)S(1)}, bf16[1536,768]{1,0:T(8,128)(2,1)}, u32[]{:S(2)}) copy-start(bf16[1536,768]{1,0:T(8,128)(2,1)} %wo_ref.2) | copy-start | bytes 7077892
  3.0 30.1 %collective-permute-start = (bf16[384,1152]{1,0:T(8,128)(2,1)}, bf16[384,1152]{1,0:T(8,128)(2,1)}, u32[]{:S(2)}, u32[]{:S(2)}) collective-permute-start(bf16[384,1152]{1,0:T(8,128)(2,1)} %fusion.19), channel_id=1, source_target_pairs={{0,1},{1,0},{2,3},{3,2},{4,5},{5,4},{6,7},{7,6},{8,9},{9,8},{10,11... | collective-permute-start | bytes 2654216 | tf_op jit(solution)/shard_map/ppermute | solution.py:378
  5.9 5.4 %copy-start.9 = (bf16[16,32]{1,0:T(8,128)(2,1)}, bf16[16,32]{1,0:T(8,128)(2,1)S(1)}, u32[]{:S(2)}) copy-start(bf16[16,32]{1,0:T(8,128)(2,1)S(1)} %pad.4.table_ref) | copy-start | bytes 3076
  5.9 80.5 %collective-permute-start.4 = (bf16[16,32]{1,0:T(8,128)(2,1)S(1)}, bf16[16,32]{1,0:T(8,128)(2,1)S(1)}, u32[]{:S(2)}, u32[]{:S(2)}) collective-permute-start(bf16[16,32]{1,0:T(8,128)(2,1)S(1)} %pad.4.table_ref), channel_id=1, source_target_pairs={{0,1},{1,0},{2,3},{3,2},{4,5},{5,4},{6,7},{7,6},{8,9},{9,8},{10,11... | collective-permute-start | bytes 3080 | tf_op jit(solution)/shard_map/ppermute | solution.py:378
  6.8 26.3 %collective-permute-start.2 = (bf16[192,768]{1,0:T(8,128)(2,1)}, bf16[192,768]{1,0:T(8,128)(2,1)}, u32[]{:S(2)}, u32[]{:S(2)}) collective-permute-start(bf16[192,768]{1,0:T(8,128)(2,1)} %constant_dynamic-slice_fusion.2), channel_id=1, source_target_pairs={{0,1},{1,0},{2,3},{3,2},{4,5},{5,4},{6,7},{7,6},{8,9},{9,8},{10,11... | collective-permute-start | bytes 884744 | tf_op jit(solution)/shard_map/ppermute | solution.py:378
  8.9 27.9 %copy-start.12 = (bf16[768]{0:T(1024)(128)(2,1)S(1)}, bf16[768]{0:T(1024)(128)(2,1)}, u32[]{:S(2)}) copy-start(bf16[768]{0:T(1024)(128)(2,1)} %param.13) | copy-start | bytes 4612
  8.9 28.5 %copy-start.13 = (bf16[768]{0:T(1024)(128)(2,1)S(1)}, bf16[768]{0:T(1024)(128)(2,1)}, u32[]{:S(2)}) copy-start(bf16[768]{0:T(1024)(128)(2,1)} %param.19) | copy-start | bytes 4612
  8.9 49.8 %collective-permute-start.7 = (bf16[768,768]{1,0:T(8,128)(2,1)S(1)}, bf16[768,768]{1,0:T(8,128)(2,1)S(1)}, u32[]{:S(2)}, u32[]{:S(2)}) collective-permute-start(bf16[768,768]{1,0:T(8,128)(2,1)S(1)} %constant_dynamic-slice_fusion), channel_id=1, source_target_pairs={{0,1},{1,0},{2,3},{3,2},{4,5},{5,4},{6,7},{7,6},{8,9},{9,8},{10,11... | collective-permute-start | bytes 3538952 | tf_op jit(solution)/shard_map/ppermute | solution.py:378
  11.3 71.4 %collective-permute-start.5 = (bf16[384,1536]{1,0:T(8,128)(2,1)}, bf16[384,1536]{1,0:T(8,128)(2,1)S(1)}, u32[]{:S(2)}, u32[]{:S(2)}) collective-permute-start(bf16[384,1536]{1,0:T(8,128)(2,1)} %constant_dynamic-slice_fusion.1), channel_id=1, source_target_pairs={{0,1},{1,0},{2,3},{3,2},{4,5},{5,4},{6,7},{7,6},{8,9},{9,8},{10,11... | collective-permute-start | bytes 3538952 | tf_op jit(solution)/shard_map/ppermute | solution.py:378
  33.1 23.4 %collective-permute-start.3 = (bf16[192,768]{1,0:T(8,128)(2,1)}, bf16[192,768]{1,0:T(8,128)(2,1)}, u32[]{:S(2)}, u32[]{:S(2)}) collective-permute-start(bf16[192,768]{1,0:T(8,128)(2,1)} %collective-permute-done.2), channel_id=1, source_target_pairs={{0,2},{2,0},{4,6},{6,4},{8,10},{10,8},{12,14},{14,12},{16,18},{18,... | collective-permute-start | bytes 884744 | tf_op jit(solution)/shard_map/ppermute | solution.py:375
  33.1 49.6 %collective-permute-start.1 = (bf16[384,1152]{1,0:T(8,128)(2,1)}, bf16[384,1152]{1,0:T(8,128)(2,1)}, u32[]{:S(2)}, u32[]{:S(2)}) collective-permute-start(bf16[384,1152]{1,0:T(8,128)(2,1)} %collective-permute-done), channel_id=1, source_target_pairs={{0,2},{2,0},{4,6},{6,4},{8,10},{10,8},{12,14},{14,12},{16,18},{18,... | collective-permute-start | bytes 2654216 | tf_op jit(solution)/shard_map/ppermute | solution.py:375
  58.7 74.6 %collective-permute-start.8 = (bf16[768,768]{1,0:T(8,128)(2,1)S(1)}, bf16[768,768]{1,0:T(8,128)(2,1)S(1)}, u32[]{:S(2)}, u32[]{:S(2)}) collective-permute-start(bf16[768,768]{1,0:T(8,128)(2,1)S(1)} %collective-permute-done.7), channel_id=1, source_target_pairs={{0,2},{2,0},{4,6},{6,4},{8,10},{10,8},{12,14},{14,12},{16,18},{18,... | collective-permute-start | bytes 3538952 | tf_op jit(solution)/shard_map/ppermute | solution.py:375
  82.7 52.3 %collective-permute-start.6 = (bf16[384,1536]{1,0:T(8,128)(2,1)S(1)}, bf16[384,1536]{1,0:T(8,128)(2,1)}, u32[]{:S(2)}, u32[]{:S(2)}) collective-permute-start(bf16[384,1536]{1,0:T(8,128)(2,1)S(1)} %collective-permute-done.5), channel_id=1, source_target_pairs={{0,2},{2,0},{4,6},{6,4},{8,10},{10,8},{12,14},{14,12},{16,18},{18,... | collective-permute-start | bytes 3538952 | tf_op jit(solution)/shard_map/ppermute | solution.py:375
  86.5 0.6 copy-start.14
  171.6 45.4 %collective-permute-start.23 = (bf16[2,384,1536]{2,1,0:T(8,128)(2,1)}, bf16[2,384,1536]{2,1,0:T(8,128)(2,1)S(1)}, u32[]{:S(2)}, u32[]{:S(2)}) collective-permute-start(bf16[2,384,1536]{2,1,0:T(8,128)(2,1)} %get-tuple-element.84), channel_id=1, source_target_pairs={{0,2},{2,0},{4,6},{6,4},{8,10},{10,8},{12,14},{14,12},{16,18},{18,... | collective-permute-start | bytes 7077896 | tf_op jit(solution)/shard_map/ppermute | solution.py:375
  193.3 28.6 %collective-permute-start.16 = (bf16[384,1536]{1,0:T(8,128)(2,1)}, bf16[384,1536]{1,0:T(8,128)(2,1)S(1)}, u32[]{:S(2)}, u32[]{:S(2)}) collective-permute-start(bf16[384,1536]{1,0:T(8,128)(2,1)} %get-tuple-element.80), channel_id=1, source_target_pairs={{0,2},{2,0},{4,6},{6,4},{8,10},{10,8},{12,14},{14,12},{16,18},{18,... | collective-permute-start | bytes 3538952 | tf_op jit(solution)/shard_map/ppermute | solution.py:375
  193.3 127.7 %collective-permute-start.22 = (bf16[2,384,1536]{2,1,0:T(8,128)(2,1)}, bf16[2,384,1536]{2,1,0:T(8,128)(2,1)}, u32[]{:S(2)}, u32[]{:S(2)}) collective-permute-start(bf16[2,384,1536]{2,1,0:T(8,128)(2,1)} %get-tuple-element.82), channel_id=1, source_target_pairs={{0,2},{2,0},{4,6},{6,4},{8,10},{10,8},{12,14},{14,12},{16,18},{18,... | collective-permute-start | bytes 7077896 | tf_op jit(solution)/shard_map/ppermute | solution.py:375
  193.8 44.9 %collective-permute-start.10 = (f32[32,6]{1,0:T(8,128)}, f32[32,6]{1,0:T(8,128)S(1)}, u32[]{:S(2)}, u32[]{:S(2)}) collective-permute-start(f32[32,6]{1,0:T(8,128)} %bitcast.45), channel_id=1, source_target_pairs={{0,1},{1,0},{2,3},{3,2},{4,5},{5,4},{6,7},{7,6},{8,9},{9,8},{10,11... | collective-permute-start | bytes 2312 | tf_op jit(solution)/shard_map/ppermute | solution.py:378
  216.9 99.1 %collective-permute-start.15 = (bf16[384,1536]{1,0:T(8,128)(2,1)}, bf16[384,1536]{1,0:T(8,128)(2,1)}, u32[]{:S(2)}, u32[]{:S(2)}) collective-permute-start(bf16[384,1536]{1,0:T(8,128)(2,1)} %get-tuple-element.78), channel_id=1, source_target_pairs={{0,2},{2,0},{4,6},{6,4},{8,10},{10,8},{12,14},{14,12},{16,18},{18,... | collective-permute-start | bytes 3538952 | tf_op jit(solution)/shard_map/ppermute | solution.py:375
  217.0 1.4 copy-start
  218.4 4.5 %copy-start.2 = (bf16[384,1536]{1,0:T(8,128)(2,1)S(1)}, bf16[384,1536]{1,0:T(8,128)(2,1)}, u32[]{:S(2)}) copy-start(bf16[384,1536]{1,0:T(8,128)(2,1)} %get-tuple-element.79) | copy-start | bytes 3538948
  221.5 99.5 %collective-permute-start.24 = (bf16[2,384,1536]{2,1,0:T(8,128)(2,1)S(1)}, bf16[2,384,1536]{2,1,0:T(8,128)(2,1)}, u32[]{:S(2)}, u32[]{:S(2)}) collective-permute-start(bf16[2,384,1536]{2,1,0:T(8,128)(2,1)S(1)} %add_convert_fusion.1), channel_id=1, source_target_pairs={{0,1},{1,0},{2,3},{3,2},{4,5},{5,4},{6,7},{7,6},{8,9},{9,8},{10,11... | collective-permute-start | bytes 7077896 | tf_op jit(solution)/shard_map/ppermute | solution.py:378
  221.9 1.0 copy-start.3
  224.4 91.7 %collective-permute-start.17 = (bf16[384,1536]{1,0:T(8,128)(2,1)S(1)}, bf16[384,1536]{1,0:T(8,128)(2,1)}, u32[]{:S(2)}, u32[]{:S(2)}) collective-permute-start(bf16[384,1536]{1,0:T(8,128)(2,1)S(1)} %add_convert_fusion.4), channel_id=1, source_target_pairs={{0,1},{1,0},{2,3},{3,2},{4,5},{5,4},{6,7},{7,6},{8,9},{9,8},{10,11... | collective-permute-start | bytes 3538952 | tf_op jit(solution)/shard_map/ppermute | solution.py:378
  226.2 11.9 %copy-start.10 = (f32[1,768]{1,0:T(1,128)S(1)}, f32[1,768]{1,0:T(1,128)}, u32[]{:S(2)}) copy-start(f32[1,768]{1,0:T(1,128)} %get-tuple-element.74) | copy-start | bytes 9220
  226.2 13.1 %copy-start.8 = (f32[32,128]{1,0:T(8,128)S(1)}, f32[32,128]{1,0:T(8,128)}, u32[]{:S(2)}) copy-start(f32[32,128]{1,0:T(8,128)} %get-tuple-element.75) | copy-start | bytes 49156
  238.7 0.6 copy-start.7
  238.7 62.0 %collective-permute-start.9 = (f32[1,1536]{1,0:T(1,128)}, f32[1,1536]{1,0:T(1,128)}, u32[]{:S(2)}, u32[]{:S(2)}) collective-permute-start(f32[1,1536]{1,0:T(1,128)} %constant_dynamic-update-slice_fusion), channel_id=1, source_target_pairs={{0,1},{1,0},{2,3},{3,2},{4,5},{5,4},{6,7},{7,6},{8,9},{9,8},{10,11... | collective-permute-start | bytes 18440 | tf_op jit(solution)/shard_map/ppermute | solution.py:378
  302.1 1.2 collective-permute-start.11
  304.0 3.7 collective-permute-start.12
  307.7 3.7 collective-permute-start.13
  311.4 4.6 %collective-permute-start.14 = (f32[1,1728]{1,0:T(1,128)S(1)}, f32[1,1728]{1,0:T(1,128)S(1)}, u32[]{:S(2)}, u32[]{:S(2)}) collective-permute-start(f32[1,1728]{1,0:T(1,128)S(1)} %add.122), channel_id=1, source_target_pairs={{0,16},{2,18},{4,20},{6,22},{8,24},{10,26},{12,28},{14,30},{16,0},... | collective-permute-start | bytes 20744 | tf_op jit(solution)/shard_map/ppermute | solution.py:375
  316.1 9.9 %copy-start.6 = (f32[1,1728]{1,0:T(1,128)}, f32[1,1728]{1,0:T(1,128)S(1)}, u32[]{:S(2)}) copy-start(f32[1,1728]{1,0:T(1,128)S(1)} %add.123) | copy-start | bytes 20740
  316.1 5.0 %copy-start.1 = (bf16[2,384,1536]{2,1,0:T(8,128)(2,1)S(1)}, bf16[2,384,1536]{2,1,0:T(8,128)(2,1)}, u32[]{:S(2)}) copy-start(bf16[2,384,1536]{2,1,0:T(8,128)(2,1)} %get-tuple-element.81) | copy-start | bytes 7077892
  319.5 16.6 %collective-permute-start.18 = (bf16[192,1536]{1,0:T(8,128)(2,1)}, bf16[192,1536]{1,0:T(8,128)(2,1)}, u32[]{:S(2)}, u32[]{:S(2)}) collective-permute-start(bf16[192,1536]{1,0:T(8,128)(2,1)} %slice.115), channel_id=1, source_target_pairs={{0,4},{2,6},{4,0},{6,2},{8,12},{10,14},{12,8},{14,10},{16,20},{18,... | collective-permute-start | bytes 1769480 | tf_op jit(solution)/shard_map/ppermute | solution.py:375
  325.5 31.6 %collective-permute-start.25 = (bf16[2,192,1536]{2,1,0:T(8,128)(2,1)}, bf16[2,192,1536]{2,1,0:T(8,128)(2,1)}, u32[]{:S(2)}, u32[]{:S(2)}) collective-permute-start(bf16[2,192,1536]{2,1,0:T(8,128)(2,1)} %slice_bitcast_fusion), channel_id=1, source_target_pairs={{0,4},{2,6},{4,0},{6,2},{8,12},{10,14},{12,8},{14,10},{16,20},{18,... | collective-permute-start | bytes 3538952 | tf_op jit(solution)/shard_map/ppermute | solution.py:375
  337.3 25.5 %collective-permute-start.19 = (bf16[48,1536]{1,0:T(8,128)(2,1)S(1)}, bf16[48,1536]{1,0:T(8,128)(2,1)S(1)}, u32[]{:S(2)}, u32[]{:S(2)}) collective-permute-start(bf16[48,1536]{1,0:T(8,128)(2,1)S(1)} %get-tuple-element.117), channel_id=1, source_target_pairs={{0,8},{2,10},{4,12},{6,14},{8,0},{10,2},{12,4},{14,6},{16,24},{18,... | collective-permute-start | bytes 442376 | tf_op jit(solution)/shard_map/ppermute | solution.py:375
  339.0 23.9 %collective-permute-start.21 = (bf16[48,1536]{1,0:T(8,128)(2,1)S(1)}, bf16[48,1536]{1,0:T(8,128)(2,1)S(1)}, u32[]{:S(2)}, u32[]{:S(2)}) collective-permute-start(bf16[48,1536]{1,0:T(8,128)(2,1)S(1)} %get-tuple-element.118), channel_id=1, source_target_pairs={{0,24},{2,26},{4,28},{6,30},{8,16},{10,18},{12,20},{14,22},{16,8},... | collective-permute-start | bytes 442376 | tf_op jit(solution)/shard_map/ppermute | solution.py:375
  341.5 21.5 %collective-permute-start.20 = (bf16[48,1536]{1,0:T(8,128)(2,1)S(1)}, bf16[48,1536]{1,0:T(8,128)(2,1)S(1)}, u32[]{:S(2)}, u32[]{:S(2)}) collective-permute-start(bf16[48,1536]{1,0:T(8,128)(2,1)S(1)} %get-tuple-element.119), channel_id=1, source_target_pairs={{0,16},{2,18},{4,20},{6,22},{8,24},{10,26},{12,28},{14,30},{16,0},... | collective-permute-start | bytes 442376 | tf_op jit(solution)/shard_map/ppermute | solution.py:375
  358.7 11.3 %collective-permute-start.26 = (bf16[2,48,1536]{2,1,0:T(8,128)(2,1)S(1)}, bf16[2,48,1536]{2,1,0:T(8,128)(2,1)S(1)}, u32[]{:S(2)}, u32[]{:S(2)}) collective-permute-start(bf16[2,48,1536]{2,1,0:T(8,128)(2,1)S(1)} %get-tuple-element.112), channel_id=1, source_target_pairs={{0,8},{2,10},{4,12},{6,14},{8,0},{10,2},{12,4},{14,6},{16,24},{18,... | collective-permute-start | bytes 884744 | tf_op jit(solution)/shard_map/ppermute | solution.py:375
  360.3 14.7 %collective-permute-start.28 = (bf16[2,48,1536]{2,1,0:T(8,128)(2,1)S(1)}, bf16[2,48,1536]{2,1,0:T(8,128)(2,1)S(1)}, u32[]{:S(2)}, u32[]{:S(2)}) collective-permute-start(bf16[2,48,1536]{2,1,0:T(8,128)(2,1)S(1)} %get-tuple-element.113), channel_id=1, source_target_pairs={{0,24},{2,26},{4,28},{6,30},{8,16},{10,18},{12,20},{14,22},{16,8},... | collective-permute-start | bytes 884744 | tf_op jit(solution)/shard_map/ppermute | solution.py:375
  362.8 21.8 %collective-permute-start.27 = (bf16[2,48,1536]{2,1,0:T(8,128)(2,1)S(1)}, bf16[2,48,1536]{2,1,0:T(8,128)(2,1)S(1)}, u32[]{:S(2)}, u32[]{:S(2)}) collective-permute-start(bf16[2,48,1536]{2,1,0:T(8,128)(2,1)S(1)} %get-tuple-element.114), channel_id=1, source_target_pairs={{0,16},{2,18},{4,20},{6,22},{8,24},{10,26},{12,28},{14,30},{16,0},... | collective-permute-start | bytes 884744 | tf_op jit(solution)/shard_map/ppermute | solution.py:375
